TPU v7x, 512 devices: a whole 4x4x16 slice. The times are simulated.
512 devices in a mesh: seq: 64 (over z_hi, y, x, core), head: 8 (over z_lo).
Axes of the slice: x: 4, y: 4, z: 16 (z_hi: 2, z_lo: 8; z = z_hi * 8 + z_lo), core: 2. Of those that a mesh axis runs over, the one named last changes fastest.
Arguments:
- clean_query: bfloat16 [512, 5120], P('seq', 'head'), may hold values from -80 to 80
- noise: bfloat16 [512, 5120], P('seq', 'head'), may hold values from -4 to 4
- key_cache: bfloat16 [131072, 1024], P('seq', 'head'), may hold values from -10.5 to 10.5
- value_cache: bfloat16 [131072, 1024], P('seq', 'head'), may hold values from -10 to 10
- out_weight: bfloat16 [5120, 5120], P('head', 'seq'), may hold values from -0.078125 to 0.078125
- row_run: int32 [512], replicated, may hold values from 0 to 15, as said below
- limits: int32 [512], replicated, may hold values from 65 to 131072, as said below
- restored: int32 [16], replicated, may hold values from 64 to 131071, as said below
Outputs:
- traced: bfloat16 [512, 5120], P('head', 'seq')
Inputs may be any that keep to these rules, and one draw needn't show every extreme that they name: `row_run`: each run owns exactly 32 rows, in any order. The rows of one run have the limits s + 1 to s + 32 for a start s of that run. restored[r] is limits[i] - 1 of one row i of run r.
All inputs are finite; a program needn't handle non-finite values.
Results may differ from a plain program's by a relative error of at most 0.019.
Values may be sent and summed in bfloat16 or wider, within the bound.
A program may use at most 192 MiB of HBM per device.

v0:
```python
import math

import jax
import jax.numpy as jnp
from jax import lax
from jax.sharding import PartitionSpec as P

HD = 128


NEG_FILL = -1e30


def corrupt_rows(clean_query, noise, row_run, limits, restored, first_row):
    row_count = clean_query.shape[0]
    run_ids = lax.dynamic_slice_in_dim(row_run, first_row, row_count, 0)
    row_limits = lax.dynamic_slice_in_dim(limits, first_row, row_count, 0)
    run_table = run_ids[:, None] == jnp.arange(restored.shape[0], dtype=jnp.int32)[None, :]
    restored_row = jnp.sum(jnp.where(run_table, restored[None, :], 0), axis=1)
    keep_noise = jnp.where(row_limits - 1 == restored_row, 0.0, 1.0).astype(jnp.float32)
    mixed = clean_query.astype(jnp.float32) + noise.astype(jnp.float32) * keep_noise[:, None]
    return mixed.astype(jnp.bfloat16)


def shard_attention(block_queries, block_limits, key_block, value_block, shard_start):
    row_count = block_queries.shape[0]
    kv_local = key_block.shape[1]
    head_dim = key_block.shape[2]
    group_size = block_queries.shape[1] // (kv_local * head_dim)
    grouped = block_queries.reshape(row_count, kv_local, group_size, head_dim)
    scores = jnp.einsum("rkgd,ckd->rkgc", grouped, key_block, preferred_element_type=jnp.float32)
    scores = scores * (1.0 / math.sqrt(head_dim))
    position = shard_start + jnp.arange(key_block.shape[0], dtype=jnp.int32)
    allowed = position[None, None, None, :] < block_limits[:, None, None, None]
    masked = jnp.where(allowed, scores, NEG_FILL)
    row_top = jnp.max(masked, axis=3)
    exps = jnp.where(allowed, jnp.exp(masked - row_top[..., None]), 0.0)
    row_total = jnp.sum(exps, axis=3)
    weighted = jnp.einsum(
        "rkgc,ckd->rkgd", exps.astype(jnp.bfloat16), value_block, preferred_element_type=jnp.float32
    )
    stat_cols = kv_local * group_size
    return (
        row_top.reshape(row_count, stat_cols),
        row_total.reshape(row_count, stat_cols),
        weighted.reshape(row_count, stat_cols * head_dim),
    )


def local_attention(gathered, limits, key_block, value_block, shard_start):
    row_count, width = gathered.shape
    block_rows = math.gcd(row_count, 64)
    block_count = row_count // block_rows
    stat_cols = width // key_block.shape[2]

    def one_block(pieces):
        block_queries, block_limits = pieces
        return shard_attention(block_queries, block_limits, key_block, value_block, shard_start)

    results = lax.map(
        one_block,
        (gathered.reshape(block_count, block_rows, width), limits.reshape(block_count, block_rows)),
    )
    return (
        results[0].reshape(row_count, stat_cols),
        results[1].reshape(row_count, stat_cols),
        results[2].reshape(row_count, width),
    )


def shards(clean_query, noise, key_cache, value_cache, out_weight, row_run, limits, restored):
    seq_index = lax.axis_index("seq")
    local_rows = clean_query.shape[0]
    shard_len = key_cache.shape[0]
    shard_start = seq_index * shard_len
    head_dim = HD
    kv_local = key_cache.shape[1] // head_dim
    key_block = key_cache.reshape(shard_len, kv_local, head_dim)
    value_block = value_cache.reshape(shard_len, kv_local, head_dim)
    queries = corrupt_rows(clean_query, noise, row_run, limits, restored, seq_index * local_rows)
    gathered = lax.all_gather(queries, "seq", axis=0, tiled=True)
    row_top, row_total, weighted = local_attention(
        gathered, limits, key_block, value_block, shard_start
    )
    global_top = lax.pmax(row_top, "seq")
    factor = jnp.exp(row_top - global_top)
    total_sum, value_sum = lax.psum(
        (row_total * factor, weighted * jnp.repeat(factor, head_dim, axis=1)), "seq"
    )
    attended = (value_sum / jnp.repeat(total_sum, head_dim, axis=1)).astype(jnp.bfloat16)
    return lax.psum_scatter(
        jnp.dot(attended, out_weight, preferred_element_type=jnp.float32).astype(jnp.bfloat16),
        "head",
        scatter_dimension=0,
        tiled=True,
    )


def solution(mesh):
    placed = (
        P("seq", "head"),
        P("seq", "head"),
        P("seq", "head"),
        P("seq", "head"),
        P("head", "seq"),
        P(),
        P(),
        P(),
    )
    return jax.shard_map(
        shards, mesh=mesh, in_specs=placed, out_specs=P("head", "seq"), check_vma=False
    )
```

profile of v0, /device:TPU:6, one launch (start us, length us, event | category | flops | bytes accessed | tf_op | source)
XLA Modules:
  0.0 1909.2 jit_solution(12580269928795100662)
XLA Ops:
  6.5 0.8 reshape.102
  7.3 0.8 dynamic_slice.15
  8.1 0.8 select_reduce_fusion
  8.9 0.8 compare_select_fusion
  9.7 0.8 add_convert_fusion
  10.5 145.0 %all_gather.3 = bf16[512,640]{1,0:T(8,128)(2,1)} all-gather(bf16[8,640]{1,0:T(8,128)(2,1)S(1)} %add_convert_fusion), channel_id=1, replica_groups=mesh['seq'=64,'head'=8] {'seq'}, dimensions={0}, use_global_device_ids=true | all-gather | bytes 665600 | tf_op jit(solution)/shard_map/all_gather | solution.py:81
  155.5 43.3 %while.14 = (s32[]{:T(128)}, f32[8,64,5]{1,0,2:T(8,128)S(1)}, f32[8,64,5]{1,0,2:T(8,128)S(1)}, f32[8,64,640]{2,1,0:T(8,128)}, s32[]{:T(128)}, /*index=5*/s32[8,6...) while((s32[]{:T(128)}, f32[8,64,5]{1,0,2:T(8,128)S(1)}, ...), condition=%wide.region_4.5_spmd, body=%wide.region_1.4_spmd.sunk | while | flops 341575040 | bytes 13123497 | solution.py:60
  155.5 0.9 constant_dynamic-slice_fusion.3
  156.7 1.7 fusion.30
  158.5 0.6 fusion.31
  160.2 0.7 constant_dynamic-update-slice_fusion.2
  160.9 0.9 constant_dynamic-slice_fusion.3
  162.1 1.7 fusion.30
  163.9 0.6 fusion.31
  164.9 0.6 fusion.32
  165.7 0.7 constant_dynamic-update-slice_fusion.2
  166.3 0.9 constant_dynamic-slice_fusion.3
  167.5 1.7 fusion.30
  169.3 0.6 fusion.31
  170.3 0.6 fusion.32
  171.1 0.7 constant_dynamic-update-slice_fusion.2
  171.7 0.9 constant_dynamic-slice_fusion.3
  172.9 1.7 fusion.30
  174.7 0.6 fusion.31
  176.5 0.7 constant_dynamic-update-slice_fusion.2
  177.1 0.9 constant_dynamic-slice_fusion.3
  178.3 1.7 fusion.30
  180.1 0.6 fusion.31
  181.9 0.7 constant_dynamic-update-slice_fusion.2
  182.5 0.9 constant_dynamic-slice_fusion.3
  183.7 1.7 fusion.30
  185.5 0.6 fusion.31
  187.3 0.7 constant_dynamic-update-slice_fusion.2
  188.0 0.9 constant_dynamic-slice_fusion.3
  189.2 1.7 fusion.30
  190.9 0.6 fusion.31
  192.7 0.7 constant_dynamic-update-slice_fusion.2
  193.4 0.9 constant_dynamic-slice_fusion.3
  194.6 1.7 fusion.30
  196.3 0.6 fusion.31
  197.4 0.6 fusion.32
  198.1 0.7 constant_dynamic-update-slice_fusion.2
  199.0 536.6 %pmax.7 = f32[512,5]{0,1:T(8,128)S(1)} all-reduce(f32[512,5]{0,1:T(8,128)S(1)} %reshape.107), channel_id=1, replica_groups=mesh['seq'=64,'head'=8] {'seq'}, use_global_device_ids=true, to_apply=%region_5.6 | all-reduce | flops 2560 | bytes 20480 | tf_op jit(solution)/shard_map/pmax | solution.py:85
  736.1 2.6 bitcast_multiply_fusion
  738.8 553.9 %psum.15 = f32[512,5]{0,1:T(8,128)S(1)} all-reduce(f32[512,5]{0,1:T(8,128)S(1)} %get-tuple-element.84), channel_id=1, replica_groups=mesh['seq'=64,'head'=8] {'seq'}, use_global_device_ids=true, to_apply=%region_7.8 | all-reduce | flops 2560 | bytes 20480 | tf_op jit(solution)/shard_map/psum | solution.py:87
  1293.3 518.8 %all-reduce.2.cloned.1.call-done = f32[512,640]{1,0:T(8,128)} async-done(((f32[512,640]{1,0:T(8,128)}), f32[512,640]{1,0:T(8,128)}) %all-reduce.2.cloned.1.call-update) | async-done | bytes 1310736 | tf_op jit(solution)/shard_map/psum | solution.py:87
  1812.1 2.3 convolution_convert_fusion
  1814.5 87.9 %reduce-scatter.2.cloned.1.call-done = bf16[64,80]{1,0:T(8,128)(2,1)} async-done(((bf16[512,80]{1,0:T(8,128)(2,1)}), bf16[64,80]{1,0:T(8,128)(2,1)}) %reduce-scatter.2.cloned.1.call-update) | async-done | bytes 10256 | tf_op jit(solution)/shard_map/reduce_scatter | solution.py:91
  (117 shorter events, 11.2 us)
Async XLA Ops:
  6.5 1805.6 %copy-start = (bf16[640,80]{0,1:T(8,128)(2,1)S(1)}, bf16[640,80]{0,1:T(8,128)(2,1)}, u32[]{:S(2)}) copy-start(bf16[640,80]{0,1:T(8,128)(2,1)} %param.14) | copy-start | bytes 307204
  6.5 1805.6 %all-reduce.2.cloned.1.call-start = ((), (), s32[]{:S(2)}) async-start(), calls=%async_computation.1 | async-start | bytes 2621440 | tf_op jit(solution)/shard_map/psum | solution.py:87
  158.5 1.0 copy-start.1
  163.9 1.0 copy-start.1
  169.3 1.0 copy-start.1
  174.7 1.0 copy-start.1
  180.1 1.0 copy-start.1
  185.5 1.0 copy-start.1
  190.9 1.0 copy-start.1
  196.3 1.0 copy-start.1
  738.7 1163.6 %reduce-scatter.2.cloned.1.call-start = ((), (), s32[]{:S(2)}) async-start(), calls=%async_computation.2 | async-start | bytes 147456 | tf_op jit(solution)/shard_map/reduce_scatter | solution.py:91
Sparse Core Ops, SparseCore 0:
  738.9 1073.1 all-reduce.1
  1815.1 87.1 reduce-scatter.1
where the time goes:
time: 1910 us
  blocking collectives  1240 us (65%)
  waiting for transfers between devices  607 us (32%)
  local copies, waits for them, and re-layouts  21.1 us (1%)
  matrix products  20.6 us (1%)
    psum x1, blocking collectives, shards(): lax.psum((row_total * factor, weighted * jnp.repeat(factor, head_dim, axi...  554 us
    pmax x1, blocking collectives, shards(): global_top = lax.pmax(row_top, 'seq')  537 us
    psum x1, waiting for transfers between devices, shards(): lax.psum((row_total * factor, weighted * jnp.repeat(factor, head_dim, axi...  519 us
    all_gather x1, blocking collectives, shards(): gathered = lax.all_gather(queries, 'seq', axis=0, tiled=True)  145 us
    reduce_scatter x1, waiting for transfers between devices, shards(): lax.psum_scatter(jnp.dot(attended, out_weight, preferred_element_type=jnp...  87.9 us
  transfers between devices with their start and end apart: 2, of which 2 were waited for; matrix products, arithmetic and copies ran while one was open for 0% of the time, Pallas kernels for 0%

commit v1 on v0

v1 whole, which is shorter than its diff:
```python
import functools
import math

import jax
import jax.numpy as jnp
from jax import lax
from jax.experimental import pallas as pl
from jax.experimental.pallas import tpu as pltpu
from jax.sharding import PartitionSpec as P

MESH = pl.DeviceIdType.MESH
F32 = jnp.float32
BF16 = jnp.bfloat16

HD = 128
GROUP = 5
SCALE = math.log2(math.e) / math.sqrt(HD)
MASKED = -1e30
BLOCK = 16 * GROUP
PACK = BLOCK + 16
CHUNK = 4 * BLOCK
SUB = CHUNK // 2


def lanes_of(shape):
    return lax.broadcasted_iota(jnp.int32, shape, len(shape) - 1)


def pack_stat(rows):
    lane = lanes_of((16, 128))
    tile = jnp.zeros((16, 128), F32)
    for j, row in enumerate(rows):
        tile = jnp.where((lane % 8 == j) & (lane < 24), row, tile)
    high = tile.astype(BF16).astype(F32)
    rest = tile - high
    middle = rest.astype(BF16).astype(F32)
    low = rest - middle
    return jnp.where(lane < 8, high, jnp.where(lane < 16, middle, low)).astype(BF16)


def unpack_stat(tile):
    tile = tile.astype(F32)
    return tile + pltpu.roll(tile, 120, 1) + pltpu.roll(tile, 112, 1)


def head_column(tile, j):
    return jnp.broadcast_to(tile[:, j : j + 1], (16, 128))


def kernel(
    cq_ref, nz_ref, k_hbm, v_hbm, w_hbm, run_ref, lim_ref, restored_ref,
    out_ref,
    k_in, v_in, w_in, own_q, queries, rhs, v_ones, lhs, scores, probs, tops,
    partial, landed, zh_out, zh_in, attended, weights, proj_out, proj_in, limit_col, keep_col,
    load_sem, sib_sem, w_sem, zq_sem, q_send, q_recv, part_send, part_recv, zh_sem, att_send, att_recv, proj_send, proj_recv,
):
    seq, head = lax.axis_index("seq"), lax.axis_index("head")
    shard_len = k_hbm.shape[0]
    cols = w_hbm.shape[1]
    zh, chip, core = seq // 32, (seq // 2) % 16, seq % 2
    y, x = chip // 4, chip % 4

    def device(zh_, chip_, core_, head_):
        return (zh_ * 32 + chip_ * 2 + core_, head_)

    def plane_chip(i):
        return ((y + i // 4) % 4) * 4 + (x + i % 4) % 4

    sibling = device(zh, chip, 1 - core, head)
    zh_peer = device(1 - zh, chip, core, head)

    def remote(src, dst, send, recv, to):
        return pltpu.make_async_remote_copy(
            src_ref=src, dst_ref=dst, send_sem=send, recv_sem=recv, device_id=to, device_id_type=MESH
        )

    barrier = pltpu.get_barrier_semaphore()

    def greet(to):
        pl.semaphore_signal(barrier, inc=1, device_id=to, device_id_type=MESH)

    greet(zh_peer)

    def greet_head(i, _):
        greet(device(zh, chip, (core + i) % 2, (head + i // 2) % 8))
        return 0

    lax.fori_loop(2, 16, greet_head, 0)

    def greet_plane(i, _):
        greet(device(zh, plane_chip(i // 2), (core + i) % 2, head))
        return 0

    lax.fori_loop(1, 32, greet_plane, 0)

    loads = [
        pltpu.make_async_copy(src, dst, load_sem.at[i])
        for i, (src, dst) in enumerate(((k_hbm, k_in), (v_hbm, v_in), (w_hbm, w_in)))
    ]
    for load in loads:
        load.start()

    limits = lim_ref[...]
    runs = run_ref[...]
    restored = jnp.zeros(runs.shape, jnp.int32)
    for r in range(restored_ref.shape[0]):
        restored = jnp.where(runs == r, restored_ref[r], restored)
    keep = jnp.where(limits - 1 == restored, 0.0, 1.0).astype(F32)
    limits = limits.astype(F32)
    diagonal = lax.broadcasted_iota(jnp.int32, (128, 128), 0) == lanes_of((128, 128))
    for t in range(limits.shape[0]):
        for table, column in ((limits, limit_col), (keep, keep_col)):
            spread = jnp.where(diagonal, jnp.broadcast_to(table[t : t + 1, :], (128, 128)), 0.0)
            column[t * 128 : (t + 1) * 128, :] = jnp.broadcast_to(
                jnp.sum(spread, axis=1, keepdims=True), (128, 128)
            )
    my_keep = keep_col[pl.ds(pl.multiple_of(seq * 8, 8), 8), :]
    half_rows = pl.ds(pl.multiple_of(core * 8, 8), 8)
    for j in range(GROUP):
        at = slice(j * HD, (j + 1) * HD)
        own_q[j, half_rows, :] = cq_ref[:, at].astype(F32) + nz_ref[:, at].astype(F32) * my_keep

    row = lax.broadcasted_iota(jnp.int32, (CHUNK, 128), 0)
    one_hot = ((row // BLOCK) * 16 + row % 16) == lanes_of((CHUNK, 128))
    lhs[:, HD:] = jnp.where(one_hot, 1.0, 0.0).astype(BF16)
    rhs[HD + 64 :, :] = jnp.zeros((64, shard_len), BF16)
    v_ones[:, HD:] = jnp.ones((shard_len, HD), BF16)
    loads[0].wait()
    rhs[:HD, :] = k_in[...].T
    loads[1].wait()
    v_ones[:, :HD] = v_in[...]
    loads[2].wait()
    weights[core] = jnp.zeros(weights.shape[1:], BF16)
    weights[core, :, :cols] = w_in[...]

    pl.semaphore_wait(barrier, 46)

    sib_copy = remote(own_q.at[:, half_rows, :], own_q.at[:, half_rows, :], sib_sem.at[0], sib_sem.at[1], sibling)
    sib_copy.start()
    w_copy = remote(weights.at[core], weights.at[core], w_sem.at[0], w_sem.at[1], sibling)
    w_copy.start()
    other_rows = pl.ds(pl.multiple_of(8 - core * 8, 8), 8)
    remote(own_q.at[:, other_rows, :], own_q.at[:, other_rows, :], sib_sem.at[0], sib_sem.at[1], sibling).wait_recv()
    queries[0, chip] = own_q[...].reshape(BLOCK, HD).astype(BF16)
    zq_copy = remote(queries.at[0, chip], queries.at[1, chip], zq_sem.at[0], zq_sem.at[1], zh_peer)
    zq_copy.start()

    def send_queries(rel):
        def step(i, _):
            remote(
                queries.at[rel, chip], queries.at[rel, chip], q_send.at[rel, i], q_recv.at[rel, chip],
                device(zh, plane_chip(i), core, head),
            ).start()
            return 0

        lax.fori_loop(1, 16, step, 0)

    send_queries(0)

    start = (seq * shard_len).astype(F32)

    def chunk(g, _):
        rel, t = g // 4, g % 4
        row_y = (y + t + t // 2 - 2 * (t // 3)) % 4
        zh_of = (zh + rel) % 2

        def arrive(i, _):
            source = row_y * 4 + i

            @pl.when(source != chip)
            def _():
                remote(
                    queries.at[rel, source], queries.at[rel, source], q_send.at[rel, 0], q_recv.at[rel, source], sibling
                ).wait_recv()

            return 0

        lax.fori_loop(0, 4, arrive, 0)
        lhs[:, :HD] = queries[rel, pl.ds(row_y * 4, 4)].reshape(CHUNK, HD)
        first = pl.multiple_of(zh_of * 256 + row_y * 64, 64)
        limit = limit_col[pl.ds(first, 64), :] - start
        for at in range(0, shard_len, 128):
            position = (lanes_of((64, 128)) + at).astype(F32)
            rhs[HD : HD + 64, at : at + 128] = jnp.where(position < limit, 0.0, MASKED).astype(BF16)
        for i in range(4):
            if i < 2:
                scores[i] = jnp.dot(lhs[i * SUB : (i + 1) * SUB, :], rhs[...], preferred_element_type=F32)
            if 1 <= i < 3:
                part = scores[i - 1]
                top = jnp.max(part, axis=1, keepdims=True)
                tops[i - 1] = jnp.broadcast_to(top, (SUB, 128))
                probs[i - 1] = jnp.exp2((part - top) * SCALE).astype(BF16)
            if 2 <= i:
                both = jnp.dot(probs[i - 2], v_ones[...], preferred_element_type=F32)
                total = both[:, HD:]
                mean = (both[:, :HD] / total).astype(BF16)
                stat = tops[i - 2] * SCALE + jnp.log2(total)
                for b in range(2):
                    slot = row_y * 4 + (i - 2) * 2 + b
                    partial[rel, slot, :BLOCK, :] = mean[b * BLOCK : (b + 1) * BLOCK]
                    partial[rel, slot, BLOCK:, :] = pack_stat(
                        [stat[b * BLOCK + j * 16 : b * BLOCK + (j + 1) * 16] for j in range(GROUP)]
                    )

        def depart(i, _):
            owner = row_y * 4 + i
            mine = (owner == chip) & (zh_of == core)

            @pl.when(mine)
            def _():
                landed[seq % 32] = partial[rel, owner]

            @pl.when(jnp.logical_not(mine))
            def _():
                remote(
                    partial.at[rel, owner], landed.at[seq % 32], part_send.at[rel, owner], part_recv.at[seq % 32],
                    device(zh, owner, zh_of, head),
                ).start()

            return 0

        lax.fori_loop(0, 4, depart, 0)
        return 0

    lax.fori_loop(0, 3, chunk, 0)
    zq_copy.wait()
    lax.fori_loop(3, 4, chunk, 0)
    lax.fori_loop(0, 1, lambda i, c: c, 0)
    send_queries(1)
    lax.fori_loop(4, 8, chunk, 0)

    def gather_stat(i, top):
        @pl.when(i != seq % 32)
        def _():
            remote(landed.at[i], landed.at[i], part_send.at[0, 0], part_recv.at[i], sibling).wait_recv()

        return jnp.maximum(top, unpack_stat(landed[i, BLOCK:, :]))

    top = lax.fori_loop(0, 32, gather_stat, jnp.full((16, 128), 2 * MASKED, F32))

    def gather_mean(i, carry):
        total, sums = carry
        weight = jnp.exp2(unpack_stat(landed[i, BLOCK:, :]) - top)
        return total + weight, tuple(
            sums[j] + head_column(weight, j) * landed[i, j * 16 : (j + 1) * 16, :].astype(F32) for j in range(GROUP)
        )

    zero = jnp.zeros((16, 128), F32)
    total, sums = lax.fori_loop(0, 32, gather_mean, (zero, (zero,) * GROUP))
    stat = top + jnp.log2(total)
    means = [sums[j] / head_column(total, j) for j in range(GROUP)]
    for j in range(GROUP):
        zh_out[j * 16 : (j + 1) * 16, :] = means[j].astype(BF16)
    zh_out[BLOCK:, :] = pack_stat([head_column(stat, j) for j in range(GROUP)])
    zh_copy = remote(zh_out, zh_in, zh_sem.at[0], zh_sem.at[1], zh_peer)
    zh_copy.start()
    zh_copy.wait()
    other = unpack_stat(zh_in[BLOCK:, :])
    top = jnp.maximum(stat, other)
    here, there = jnp.exp2(stat - top), jnp.exp2(other - top)
    share_here, share_there = here / (here + there), there / (here + there)
    for j in range(GROUP):
        mixed = head_column(share_here, j) * means[j] + head_column(share_there, j) * zh_in[
            j * 16 : (j + 1) * 16, :
        ].astype(F32)
        attended[chip, j * 16 : (j + 1) * 16, :] = mixed.astype(BF16)

    def send_attended(i, _):
        remote(
            attended.at[chip], attended.at[chip], att_send.at[i], att_recv.at[chip],
            device(zh, plane_chip(i), core, head),
        ).start()
        return 0

    lax.fori_loop(1, 16, send_attended, 0)
    w_copy.wait_send()
    remote(weights.at[1 - core], weights.at[1 - core], w_sem.at[0], w_sem.at[1], sibling).wait_recv()

    def project(t, _):
        row_y = (y + t + t // 2 - 2 * (t // 3)) % 4
        head_of = core * 4 + row_y

        def arrive(i, _):
            source = row_y * 4 + i

            @pl.when(source != chip)
            def _():
                remote(
                    attended.at[source], attended.at[source], att_send.at[0], att_recv.at[source], sibling
                ).wait_recv()

            return 0

        lax.fori_loop(0, 4, arrive, 0)
        for side in range(2):
            acc = jnp.zeros((64, 128), F32)
            for j in range(GROUP):
                rows = attended[pl.ds(row_y * 4, 4), j * 16 : (j + 1) * 16, :].reshape(64, HD)
                acc += jnp.dot(rows, weights[side, j * HD : (j + 1) * HD, :], preferred_element_type=F32)
            proj_out[row_y, side] = acc.astype(BF16)
            mine = (head_of == head) & (core == side)

            @pl.when(mine)
            def _(side=side):
                proj_in[head] = proj_out[row_y, side]

            @pl.when(jnp.logical_not(mine))
            def _(side=side):
                remote(
                    proj_out.at[row_y, side], proj_in.at[head], proj_send.at[row_y, side], proj_recv.at[head],
                    device(zh, chip, side, head_of),
                ).start()

        return 0

    lax.fori_loop(0, 4, project, 0)

    def add_head(i, acc):
        @pl.when(jnp.logical_not((i == head) & (core == head // 4)))
        def _():
            remote(proj_in.at[i], proj_in.at[i], proj_send.at[0, 0], proj_recv.at[i], sibling).wait_recv()

        return acc + proj_in[i].astype(F32)

    result = lax.fori_loop(0, 8, add_head, jnp.zeros((64, 128), F32))
    out_ref[...] = result[:, :cols].astype(BF16)

    sib_copy.wait_send()

    def left_queries(i, _):
        for rel in range(2):
            remote(
                queries.at[rel, chip], queries.at[rel, chip], q_send.at[rel, i], q_recv.at[rel, chip], sibling
            ).wait_send()
        remote(attended.at[chip], attended.at[chip], att_send.at[i], att_recv.at[chip], sibling).wait_send()
        return 0

    lax.fori_loop(1, 16, left_queries, 0)

    def left_partials(i, _):
        for rel in range(2):

            @pl.when(jnp.logical_not((i == chip) & ((zh + rel) % 2 == core)))
            def _(rel=rel):
                remote(
                    partial.at[rel, i], landed.at[0], part_send.at[rel, i], part_recv.at[0], sibling
                ).wait_send()

        return 0

    lax.fori_loop(0, 16, left_partials, 0)

    def left_proj(i, _):
        for side in range(2):

            @pl.when(jnp.logical_not((core * 4 + i == head) & (core == side)))
            def _(side=side):
                remote(
                    proj_out.at[i, side], proj_in.at[0], proj_send.at[i, side], proj_recv.at[0], sibling
                ).wait_send()

        return 0

    lax.fori_loop(0, 4, left_proj, 0)


def shards(clean_query, noise, key_cache, value_cache, out_weight, row_run, limits, restored):
    shard_len, cols = key_cache.shape[0], out_weight.shape[1]
    vmem = pl.BlockSpec(memory_space=pltpu.VMEM)
    hbm = pl.BlockSpec(memory_space=pl.ANY)
    dma = pltpu.SemaphoreType.DMA
    return pl.pallas_call(
        kernel,
        out_shape=jax.ShapeDtypeStruct((64, cols), BF16),
        in_specs=[vmem, vmem, hbm, hbm, hbm, vmem, vmem, pl.BlockSpec(memory_space=pltpu.SMEM)],
        out_specs=vmem,
        scratch_shapes=[
            pltpu.VMEM((shard_len, HD), BF16),
            pltpu.VMEM((shard_len, HD), BF16),
            pltpu.VMEM(out_weight.shape, BF16),
            pltpu.VMEM((GROUP, 16, HD), F32),
            pltpu.VMEM((2, 16, BLOCK, HD), BF16),
            pltpu.VMEM((2 * HD, shard_len), BF16),
            pltpu.VMEM((shard_len, 2 * HD), BF16),
            pltpu.VMEM((CHUNK, 2 * HD), BF16),
            pltpu.VMEM((2, SUB, shard_len), F32),
            pltpu.VMEM((2, SUB, shard_len), BF16),
            pltpu.VMEM((2, SUB, 128), F32),
            pltpu.VMEM((2, 16, PACK, HD), BF16),
            pltpu.VMEM((32, PACK, HD), BF16),
            pltpu.VMEM((PACK, HD), BF16),
            pltpu.VMEM((PACK, HD), BF16),
            pltpu.VMEM((16, BLOCK, HD), BF16),
            pltpu.VMEM((2, GROUP * HD, 128), BF16),
            pltpu.VMEM((4, 2, 64, 128), BF16),
            pltpu.VMEM((8, 64, 128), BF16),
            pltpu.VMEM((512, 128), F32),
            pltpu.VMEM((512, 128), F32),
            dma((3,)),
            dma((2,)),
            dma((2,)),
            dma((2,)),
            dma((2, 16)),
            dma((2, 16)),
            dma((2, 16)),
            dma((32,)),
            dma((2,)),
            dma((16,)),
            dma((16,)),
            dma((4, 2)),
            dma((8,)),
        ],
        compiler_params=pltpu.CompilerParams(
            collective_id=0, has_side_effects=True, vmem_limit_bytes=40 << 20
        ),
        name="tracing",
    )(
        clean_query, noise, key_cache, value_cache, out_weight,
        row_run.reshape(4, 128), limits.reshape(4, 128), restored,
    )


def solution(mesh):
    placed = (
        P("seq", "head"),
        P("seq", "head"),
        P("seq", "head"),
        P("seq", "head"),
        P("head", "seq"),
        P(),
        P(),
        P(),
    )
    return jax.shard_map(
        shards, mesh=mesh, in_specs=placed, out_specs=P("head", "seq"), check_vma=False
    )
```

time: 1910 us -> 79.8 us (0.04)
  the two profiles are of different devices: /device:TPU:6 before, /device:TPU:17 now
where the time goes in v1:
time: 79.8 us; the launch traced here: 79.6 us
  Pallas kernels  75.7 us (95%)
  local copies, waits for them, and re-layouts  3.81 us (5%)
    pallas_call x1, Pallas kernels, shards(): pl.pallas_call(kernel, out_shape=jax.ShapeDtypeStruct((64, cols), BF16),...  75.7 us
    unnamed x16, local copies, waits for them, and re-layouts  3.81 us

profile of v1, /device:TPU:17, one launch (start us, length us, event | category | flops | bytes accessed | tf_op | source)
XLA Modules:
  0.0 79.6 jit_solution(5884553380836671141)
XLA Ops:
  0.0 0.0 copy-start.2
  0.0 0.0 copy-start.3
  0.0 0.0 copy-start.4
  0.0 0.0 copy-start.5
  0.0 0.0 copy-start.6
  0.0 1.1 %copy.9.w_hbm = bf16[640,80]{1,0:T(8,128)(2,1)S(1)} copy(bf16[640,80]{0,1:T(8,128)(2,1)} %param.12) | data formatting | bytes 204800 | tf_op args[4]
  1.1 0.0 copy-done.2
  1.1 0.0 copy-done.3
  1.2 0.0 copy-done.4
  1.2 0.0 copy-done.5
  1.2 0.0 copy-done.6
  1.2 0.0 copy-start
  1.2 1.0 %copy-done = bf16[2048,128]{1,0:T(8,128)(2,1)S(1)} copy-done((bf16[2048,128]{1,0:T(8,128)(2,1)S(1)}, bf16[2048,128]{1,0:T(8,128)(2,1)}, u32[]{:S(2)}) %copy-start) | copy-done | bytes 524312
  2.2 0.0 copy-start.1
  2.2 1.0 %copy-done.1 = bf16[2048,128]{1,0:T(8,128)(2,1)S(1)} copy-done((bf16[2048,128]{1,0:T(8,128)(2,1)S(1)}, bf16[2048,128]{1,0:T(8,128)(2,1)}, u32[]{:S(2)}) %copy-start.1) | copy-done | bytes 524312
  3.3 75.7 %tracing.1 = bf16[64,80]{1,0:T(8,128)(2,1)S(1)} custom-call(bf16[8,640]{1,0:T(8,128)(2,1)S(1)} %copy-done.2, bf16[8,640]{1,0:T(8,128)(2,1)S(1)} %copy-done.3, bf16[2048,128]{1,0:T(8,128)(2,1)S(1)} %copy-done, bf16[2048,128]{1,0:T(8,128)(2,1)S(1)} %copy-done.1, bf16[640,80]{1,0:T(8,128)(2,1)S(1)} %copy.9.w_hbm, s32[4,128]{1,0:T(4,128)S(1)} %bitcast.2, ...), custom_call_target="tpu_custom_call" | custom-call | tf_op jit(solution)/shard_map/tracing/pallas_call | solution.py:372
  79.0 0.6 copy.11
Async XLA Ops:
  0.0 1.1 %copy-start.2 = (bf16[8,640]{1,0:T(8,128)(2,1)S(1)}, bf16[8,640]{1,0:T(8,128)(2,1)}, u32[]{:S(2)}) copy-start(bf16[8,640]{1,0:T(8,128)(2,1)} %cq_ref.1) | copy-start | bytes 30724
  0.0 1.1 %copy-start.3 = (bf16[8,640]{1,0:T(8,128)(2,1)S(1)}, bf16[8,640]{1,0:T(8,128)(2,1)}, u32[]{:S(2)}) copy-start(bf16[8,640]{1,0:T(8,128)(2,1)} %nz_ref.1) | copy-start | bytes 30724
  0.0 1.1 %copy-start.4 = (s32[512]{0:T(512)S(1)}, s32[512]{0:T(512)}, u32[]{:S(2)}) copy-start(s32[512]{0:T(512)} %param.13) | copy-start | bytes 6148
  0.0 1.2 %copy-start.5 = (s32[512]{0:T(512)S(1)}, s32[512]{0:T(512)}, u32[]{:S(2)}) copy-start(s32[512]{0:T(512)} %param.14) | copy-start | bytes 6148
  0.0 1.2 %copy-start.6 = (s32[16]{0:T(128)S(1)}, s32[16]{0:T(128)}, u32[]{:S(2)}) copy-start(s32[16]{0:T(128)} %restored_ref.1) | copy-start | bytes 196
  1.2 1.0 %copy-start = (bf16[2048,128]{1,0:T(8,128)(2,1)S(1)}, bf16[2048,128]{1,0:T(8,128)(2,1)}, u32[]{:S(2)}) copy-start(bf16[2048,128]{1,0:T(8,128)(2,1)} %k_hbm.1) | copy-start | bytes 1572868
  2.2 1.0 %copy-start.1 = (bf16[2048,128]{1,0:T(8,128)(2,1)S(1)}, bf16[2048,128]{1,0:T(8,128)(2,1)}, u32[]{:S(2)}) copy-start(bf16[2048,128]{1,0:T(8,128)(2,1)} %v_hbm.1) | copy-start | bytes 1572868

commit v2 on v1

v2 whole, which is shorter than its diff:
```python
import functools
import math

import jax
import jax.numpy as jnp
from jax import lax
from jax.experimental import pallas as pl
from jax.experimental.pallas import tpu as pltpu
from jax.sharding import PartitionSpec as P

MESH = pl.DeviceIdType.MESH
F32 = jnp.float32
BF16 = jnp.bfloat16

HD = 128
GROUP = 5
SCALE = math.log2(math.e) / math.sqrt(HD)
MASKED = -1e30
BLOCK = 16 * GROUP
PACK = BLOCK + 16
CHUNK = 4 * BLOCK
SUB = CHUNK // 2


def lanes_of(shape):
    return lax.broadcasted_iota(jnp.int32, shape, len(shape) - 1)


def pack_stat(rows):
    lane = lanes_of((16, 128))
    tile = jnp.zeros((16, 128), F32)
    for j, row in enumerate(rows):
        tile = jnp.where((lane % 8 == j) & (lane < 24), row, tile)
    high = tile.astype(BF16).astype(F32)
    rest = tile - high
    middle = rest.astype(BF16).astype(F32)
    low = rest - middle
    return jnp.where(lane < 8, high, jnp.where(lane < 16, middle, low)).astype(BF16)


def unpack_stat(tile):
    tile = tile.astype(F32)
    return tile + pltpu.roll(tile, 120, 1) + pltpu.roll(tile, 112, 1)


def head_column(tile, j):
    return jnp.broadcast_to(tile[:, j : j + 1], (16, 128))


def kernel(
    cq_ref, nz_ref, k_hbm, v_hbm, w_hbm, run_ref, lim_ref, restored_ref,
    out_ref,
    k_in, v_in, own_q, queries, rhs, v_ones, lhs, scores, probs, tops,
    partial, landed, zh_out, zh_in, attended, weights_t, weights, proj_out, proj_in, limit_col, share,
    load_sem, sib_sem, w_sem, zq_sem, q_send, q_recv, part_sem, zh_sem, att_send, att_recv, proj_sem,
):
    seq, head = lax.axis_index("seq"), lax.axis_index("head")
    shard_len = k_hbm.shape[0]
    cols = w_hbm.shape[0]
    zh, chip, core = seq // 32, (seq // 2) % 16, seq % 2
    y, x = chip // 4, chip % 4

    def device(zh_, chip_, core_, head_):
        return (zh_ * 32 + chip_ * 2 + core_, head_)

    def plane_chip(i):
        return lax.rem(y + i // 4, 4) * 4 + lax.rem(x + i % 4, 4)

    sibling = device(zh, chip, 1 - core, head)
    zh_peer = device(1 - zh, chip, core, head)

    def remote(src, dst, send, recv, to):
        return pltpu.make_async_remote_copy(
            src_ref=src, dst_ref=dst, send_sem=send, recv_sem=recv, device_id=to, device_id_type=MESH
        )

    barrier = pltpu.get_barrier_semaphore()

    def greet(to):
        pl.semaphore_signal(barrier, inc=1, device_id=to, device_id_type=MESH)

    greet(zh_peer)

    for i in (4, 3, 5, 2, 6, 1, 7):
        greet(device(zh, chip, core, lax.rem(head + i, 8)))
    for i in range(15, 0, -1):
        greet(device(zh, plane_chip(i), core, head))
    greet(sibling)

    for side in range(2):
        pad = slice(side * 128 + cols, (side + 1) * 128)
        weights_t[pad, :] = jnp.zeros((128 - cols, weights_t.shape[1]), BF16)
    my_cols = weights_t.at[pl.ds(pl.multiple_of(core * 128, 128), cols), :]
    their_cols = weights_t.at[pl.ds(pl.multiple_of(128 - core * 128, 128), cols), :]
    loads = [
        pltpu.make_async_copy(src, dst, load_sem.at[i])
        for i, (src, dst) in enumerate(((k_hbm, k_in), (v_hbm, v_in), (w_hbm, my_cols)))
    ]
    for load in loads:
        load.start()

    limits = lim_ref[pl.ds(seq // 16, 1), :]
    runs = run_ref[pl.ds(seq // 16, 1), :]
    restored = jnp.zeros(runs.shape, jnp.int32)
    for r in range(restored_ref.shape[0]):
        restored = jnp.where(runs == r, restored_ref[r], restored)
    keep = jnp.where(limits - 1 == restored, 0.0, 1.0).astype(F32)
    mine = lax.broadcasted_iota(jnp.int32, (8, 128), 0) + (seq % 16) * 8 == lanes_of((8, 128))
    my_keep = jnp.sum(jnp.where(mine, jnp.broadcast_to(keep, (8, 128)), 0.0), axis=1, keepdims=True)
    half_rows = pl.ds(pl.multiple_of(core * 8, 8), 8)
    for j in range(GROUP):
        at = slice(j * HD, (j + 1) * HD)
        own_q[j, half_rows, :] = cq_ref[:, at].astype(F32) + nz_ref[:, at].astype(F32) * my_keep

    loads[2].wait()

    pl.semaphore_wait(barrier, 24)

    sib_copy = remote(own_q.at[:, half_rows, :], own_q.at[:, half_rows, :], sib_sem.at[0], sib_sem.at[1], sibling)
    sib_copy.start()
    w_copy = remote(my_cols, my_cols, w_sem.at[0], w_sem.at[1], sibling)
    w_copy.start()
    other_rows = pl.ds(pl.multiple_of(8 - core * 8, 8), 8)
    remote(own_q.at[:, other_rows, :], own_q.at[:, other_rows, :], sib_sem.at[0], sib_sem.at[1], sibling).wait_recv()
    queries[0, chip] = own_q[...].reshape(BLOCK, HD).astype(BF16)
    zq_copy = remote(queries.at[0, chip], queries.at[1, chip], zq_sem.at[0], zq_sem.at[1], zh_peer)
    zq_copy.start()

    def send_queries(rel):
        for i in range(1, 16):
            remote(
                queries.at[rel, chip], queries.at[rel, chip], q_send.at[rel], q_recv.at[rel, y],
                device(zh, plane_chip(i), core, head),
            ).start()

    send_queries(0)

    limits = lim_ref[...].astype(F32)
    diagonal = lax.broadcasted_iota(jnp.int32, (128, 128), 0) == lanes_of((128, 128))
    for t in range(limits.shape[0]):
        spread = jnp.where(diagonal, jnp.broadcast_to(limits[t : t + 1, :], (128, 128)), 0.0)
        limit_col[t * 128 : (t + 1) * 128, :] = jnp.broadcast_to(jnp.sum(spread, axis=1, keepdims=True), (128, 128))
    row = lax.broadcasted_iota(jnp.int32, (CHUNK, 128), 0)
    one_hot = ((row // BLOCK) * 16 + row % 16) == lanes_of((CHUNK, 128))
    lhs[:, HD:] = jnp.where(one_hot, 1.0, 0.0).astype(BF16)
    rhs[HD + 64 :, :] = jnp.zeros((64, shard_len), BF16)
    v_ones[:, HD:] = jnp.ones((shard_len, HD), BF16)
    loads[0].wait()
    rhs[:HD, :] = k_in[...].T
    loads[1].wait()
    v_ones[:, :HD] = v_in[...]
    w_copy.wait_send()
    remote(their_cols, their_cols, w_sem.at[0], w_sem.at[1], sibling).wait_recv()
    weights[...] = weights_t[...].T

    start = (seq * shard_len).astype(F32)

    def chunk(g, _):
        rel, t = g // 4, (g + g // 4) % 4
        row_y = (y + t + t // 2 - 2 * (t // 3)) % 4
        zh_of = (zh + rel) % 2

        def arrive(count):
            some = queries.at[rel, pl.ds(0, count)]
            remote(some, some, q_send.at[rel], q_recv.at[rel, row_y], sibling).wait_recv()

        pl.when(t == 0)(lambda: arrive(3))
        pl.when(t != 0)(lambda: arrive(4))
        lhs[:, :HD] = queries[rel, pl.ds(row_y * 4, 4)].reshape(CHUNK, HD)
        first = pl.multiple_of(zh_of * 256 + row_y * 64, 64)
        limit = limit_col[pl.ds(first, 64), :] - start
        for at in range(0, shard_len, 128):
            position = (lanes_of((64, 128)) + at).astype(F32)
            rhs[HD : HD + 64, at : at + 128] = jnp.where(position < limit, 0.0, MASKED).astype(BF16)
        for i in range(4):
            if i < 2:
                scores[i] = jnp.dot(lhs[i * SUB : (i + 1) * SUB, :], rhs[...], preferred_element_type=F32)
            if 1 <= i < 3:
                part = scores[i - 1]
                top = jnp.max(part, axis=1, keepdims=True)
                tops[i - 1] = jnp.broadcast_to(top, (SUB, 128))
                probs[i - 1] = jnp.exp2((part - top) * SCALE).astype(BF16)
            if 2 <= i:
                both = jnp.dot(probs[i - 2], v_ones[...], preferred_element_type=F32)
                total = both[:, HD:]
                mean = (both[:, :HD] / total).astype(BF16)
                stat = tops[i - 2] * SCALE + jnp.log2(total)
                for b in range(2):
                    slot = row_y * 4 + (i - 2) * 2 + b
                    partial[rel * 16 + slot, :BLOCK, :] = mean[b * BLOCK : (b + 1) * BLOCK]
                    partial[rel * 16 + slot, BLOCK:, :] = pack_stat(
                        [stat[b * BLOCK + j * 16 : b * BLOCK + (j + 1) * 16] for j in range(GROUP)]
                    )

        def depart(i, _):
            owner = row_y * 4 + i
            mine = (owner == chip) & (zh_of == core)

            @pl.when(mine)
            def _():
                landed[seq % 32] = partial[rel * 16 + owner]

            @pl.when(jnp.logical_not(mine))
            def _():
                remote(
                    partial.at[rel * 16 + owner], landed.at[seq % 32], part_sem.at[0], part_sem.at[1],
                    device(zh, owner, zh_of, head),
                ).start()

            return 0

        lax.fori_loop(0, 4, depart, 0)
        return 0

    lax.fori_loop(0, 3, chunk, 0)
    zq_copy.wait()
    send_queries(1)
    lax.fori_loop(3, 8, chunk, 0)

    all_parts = remote(partial.at[pl.ds(0, 31)], landed.at[pl.ds(0, 31)], part_sem.at[0], part_sem.at[1], sibling)
    all_parts.wait_recv()
    stats = [unpack_stat(landed[i, BLOCK:, :]) for i in range(32)]
    top = functools.reduce(jnp.maximum, stats)
    shares = [jnp.exp2(stat - top) for stat in stats]
    total = sum(shares[1:], shares[0])
    for i in range(32):
        share[i] = shares[i]

    def gather_mean(step, sums):
        for k in range(8):
            i = step * 8 + k
            weight = share[i]
            sums = tuple(
                sums[j] + head_column(weight, j) * landed[i, j * 16 : (j + 1) * 16, :].astype(F32)
                for j in range(GROUP)
            )
        return sums

    sums = lax.fori_loop(0, 4, gather_mean, (jnp.zeros((16, 128), F32),) * GROUP)
    stat = top + jnp.log2(total)
    means = [sums[j] / head_column(total, j) for j in range(GROUP)]
    for j in range(GROUP):
        zh_out[j * 16 : (j + 1) * 16, :] = means[j].astype(BF16)
    zh_out[BLOCK:, :] = pack_stat([head_column(stat, j) for j in range(GROUP)])
    zh_copy = remote(zh_out, zh_in, zh_sem.at[0], zh_sem.at[1], zh_peer)
    zh_copy.start()
    zh_copy.wait()
    other = unpack_stat(zh_in[BLOCK:, :])
    top = jnp.maximum(stat, other)
    here, there = jnp.exp2(stat - top), jnp.exp2(other - top)
    share_here, share_there = here / (here + there), there / (here + there)
    for j in range(GROUP):
        mixed = head_column(share_here, j) * means[j] + head_column(share_there, j) * zh_in[
            j * 16 : (j + 1) * 16, :
        ].astype(F32)
        attended[chip, j * 16 : (j + 1) * 16, :] = mixed.astype(BF16)

    for i in range(1, 16):
        remote(
            attended.at[chip], attended.at[chip], att_send.at[0], att_recv.at[y],
            device(zh, plane_chip(i), core, head),
        ).start()

    def project(t, _):
        row_y = (y + t + t // 2 - 2 * (t // 3)) % 4
        head_of = core * 4 + row_y

        def arrive(count):
            some = attended.at[pl.ds(0, count)]
            remote(some, some, att_send.at[0], att_recv.at[row_y], sibling).wait_recv()

        pl.when(t == 0)(lambda: arrive(3))
        pl.when(t != 0)(lambda: arrive(4))
        rows = jnp.concatenate(
            [attended[pl.ds(row_y * 4, 4), j * 16 : (j + 1) * 16, :].reshape(64, HD) for j in range(GROUP)], axis=1
        )
        both = jnp.dot(rows, weights[...], preferred_element_type=F32).astype(BF16)
        for side in range(2):
            proj_out[row_y * 2 + side] = both[:, side * 128 : (side + 1) * 128]
            mine = (head_of == head) & (core == side)

            @pl.when(mine)
            def _(side=side):
                proj_in[head] = proj_out[row_y * 2 + side]

            @pl.when(jnp.logical_not(mine))
            def _(side=side):
                remote(
                    proj_out.at[row_y * 2 + side], proj_in.at[head], proj_sem.at[0], proj_sem.at[1],
                    device(zh, chip, side, head_of),
                ).start()

        return 0

    lax.fori_loop(0, 4, project, 0)

    def proj_wait(in_half, count):
        some, into = proj_out.at[pl.ds(0, count)], proj_in.at[pl.ds(0, count)]
        copy = remote(some, into, proj_sem.at[0], proj_sem.at[1], sibling)
        pl.when(in_half)(copy.wait_recv)
        return copy.wait_send

    in_half = core == head // 4
    left_seven = proj_wait(in_half, 7)
    left_eight = proj_wait(jnp.logical_not(in_half), 8)
    result = proj_in[0].astype(F32)
    for i in range(1, 8):
        result += proj_in[i].astype(F32)
    out_ref[...] = result[:, :cols].astype(BF16)

    sib_copy.wait_send()
    for rel in range(2):
        some = queries.at[rel, pl.ds(0, 15)]
        remote(some, some, q_send.at[rel], q_recv.at[rel, 0], sibling).wait_send()
    all_parts.wait_send()
    some = attended.at[pl.ds(0, 15)]
    remote(some, some, att_send.at[0], att_recv.at[0], sibling).wait_send()
    pl.when(in_half)(left_seven)
    pl.when(jnp.logical_not(in_half))(left_eight)


def shards(clean_query, noise, key_cache, value_cache, out_weight, row_run, limits, restored):
    shard_len, cols = key_cache.shape[0], out_weight.shape[1]
    vmem = pl.BlockSpec(memory_space=pltpu.VMEM)
    hbm = pl.BlockSpec(memory_space=pltpu.HBM)
    dma = pltpu.SemaphoreType.DMA
    return pl.pallas_call(
        kernel,
        out_shape=jax.ShapeDtypeStruct((64, cols), BF16),
        in_specs=[vmem, vmem, hbm, hbm, hbm, vmem, vmem, pl.BlockSpec(memory_space=pltpu.SMEM)],
        out_specs=vmem,
        scratch_shapes=[
            pltpu.VMEM((shard_len, HD), BF16),
            pltpu.VMEM((shard_len, HD), BF16),
            pltpu.VMEM((GROUP, 16, HD), F32),
            pltpu.VMEM((2, 16, BLOCK, HD), BF16),
            pltpu.VMEM((2 * HD, shard_len), BF16),
            pltpu.VMEM((shard_len, 2 * HD), BF16),
            pltpu.VMEM((CHUNK, 2 * HD), BF16),
            pltpu.VMEM((2, SUB, shard_len), F32),
            pltpu.VMEM((2, SUB, shard_len), BF16),
            pltpu.VMEM((2, SUB, 128), F32),
            pltpu.VMEM((32, PACK, HD), BF16),
            pltpu.VMEM((32, PACK, HD), BF16),
            pltpu.VMEM((PACK, HD), BF16),
            pltpu.VMEM((PACK, HD), BF16),
            pltpu.VMEM((16, BLOCK, HD), BF16),
            pltpu.VMEM((256, GROUP * HD), BF16),
            pltpu.VMEM((GROUP * HD, 256), BF16),
            pltpu.VMEM((8, 64, 128), BF16),
            pltpu.VMEM((8, 64, 128), BF16),
            pltpu.VMEM((512, 128), F32),
            pltpu.VMEM((32, 16, 128), F32),
            dma((3,)),
            dma((2,)),
            dma((2,)),
            dma((2,)),
            dma((2,)),
            dma((2, 4)),
            dma((2,)),
            dma((2,)),
            dma((1,)),
            dma((4,)),
            dma((2,)),
        ],
        compiler_params=pltpu.CompilerParams(
            collective_id=0, has_side_effects=True, vmem_limit_bytes=60 << 20
        ),
        name="tracing",
    )(
        clean_query, noise, key_cache, value_cache, out_weight.T,
        row_run.reshape(4, 128), limits.reshape(4, 128), restored,
    )


def solution(mesh):
    placed = (
        P("seq", "head"),
        P("seq", "head"),
        P("seq", "head"),
        P("seq", "head"),
        P("head", "seq"),
        P(),
        P(),
        P(),
    )
    return jax.shard_map(
        shards, mesh=mesh, in_specs=placed, out_specs=P("head", "seq"), check_vma=False
    )
```

time: 79.8 us -> 68.7 us (0.86)
  the two profiles are of different devices: /device:TPU:17 before, /device:TPU:9 now
where the time goes in v2:
time: 68.7 us; the launch traced here: 68.5 us
  Pallas kernels  67.1 us (98%)
  local copies, waits for them, and re-layouts  1.32 us (2%)
    pallas_call x1, Pallas kernels, shards(): pl.pallas_call(kernel, out_shape=jax.ShapeDtypeStruct((64, cols), BF16),...  67.1 us

profile of v2, /device:TPU:9, one launch (start us, length us, event | category | flops | bytes accessed | tf_op | source)
XLA Modules:
  0.0 68.5 jit_solution(1175843930293793087)
XLA Ops:
  0.0 67.1 %tracing.1 = bf16[64,80]{1,0:T(8,128)(2,1)} custom-call(bf16[8,640]{1,0:T(8,128)(2,1)} %cq_ref.1, bf16[8,640]{1,0:T(8,128)(2,1)} %nz_ref.1, bf16[2048,128]{1,0:T(8,128)(2,1)} %k_hbm.1, bf16[2048,128]{1,0:T(8,128)(2,1)} %v_hbm.1, bf16[80,640]{1,0:T(8,128)(2,1)} %bitcast.3, s32[4,128]{1,0:T(4,128)} %bitcast.4, s32[4,128]{1,0:T(4,128)} %bitcast.5, s32[16]{0:T(128)} %restored_ref.1), custom_call_target="tpu_custom_call" | custom-call | tf_op jit(solution)/shard_map/tracing/pallas_call | solution.py:327
  67.2 1.3 %copy.10 = bf16[64,80]{1,0:T(8,128)(2,1)} copy(bf16[64,80]{1,0:T(8,128)(2,1)} %tracing.1) | data formatting | bytes 20480

commit v3 on v2

--- a/solution.py
+++ b/solution.py
@@ -50,9 +50,9 @@
 def kernel(
     cq_ref, nz_ref, k_hbm, v_hbm, w_hbm, run_ref, lim_ref, restored_ref,
     out_ref,
-    k_in, v_in, own_q, queries, rhs, v_ones, lhs, scores, probs, tops,
+    k_in, v_in, own_q, far_q, queries, rhs, v_ones, lhs, scores, probs, tops,
     partial, landed, zh_out, zh_in, attended, weights_t, weights, proj_out, proj_in, limit_col, share,
-    load_sem, sib_sem, w_sem, zq_sem, q_send, q_recv, part_sem, zh_sem, att_send, att_recv, proj_sem,
+    load_sem, sib_sem, w_sem, zq_send, zq_recv, q_send, q_recv, part_sem, zh_sem, att_send, att_recv, proj_sem,
 ):
     seq, head = lax.axis_index("seq"), lax.axis_index("head")
     shard_len = k_hbm.shape[0]
@@ -80,6 +80,7 @@
         pl.semaphore_signal(barrier, inc=1, device_id=to, device_id_type=MESH)
 
     greet(zh_peer)
+    greet(device(1 - zh, chip, 1 - core, head))
 
     for i in (4, 3, 5, 2, 6, 1, 7):
         greet(device(zh, chip, core, lax.rem(head + i, 8)))
@@ -107,24 +108,34 @@
     keep = jnp.where(limits - 1 == restored, 0.0, 1.0).astype(F32)
     mine = lax.broadcasted_iota(jnp.int32, (8, 128), 0) + (seq % 16) * 8 == lanes_of((8, 128))
     my_keep = jnp.sum(jnp.where(mine, jnp.broadcast_to(keep, (8, 128)), 0.0), axis=1, keepdims=True)
-    half_rows = pl.ds(pl.multiple_of(core * 8, 8), 8)
-    for j in range(GROUP):
-        at = slice(j * HD, (j + 1) * HD)
-        own_q[j, half_rows, :] = cq_ref[:, at].astype(F32) + nz_ref[:, at].astype(F32) * my_keep
+    half = 3 * HD
+    mixed = cq_ref[...].astype(F32) + nz_ref[...].astype(F32) * my_keep
+    rest = jnp.concatenate([mixed[:, half:], jnp.zeros((8, 2 * half - GROUP * HD), F32)], axis=1)
+    own_q[core] = jnp.concatenate([mixed[:, :half], rest], axis=0).astype(BF16)
 
     loads[2].wait()
 
-    pl.semaphore_wait(barrier, 24)
-
-    sib_copy = remote(own_q.at[:, half_rows, :], own_q.at[:, half_rows, :], sib_sem.at[0], sib_sem.at[1], sibling)
+    pl.semaphore_wait(barrier, 25)
+
+    zh_copies = [
+        remote(own_q.at[core], far_q.at[core], zq_send.at[side], zq_recv.at[core], device(1 - zh, chip, side, head))
+        for side in range(2)
+    ]
+    for copy in zh_copies:
+        copy.start()
+    sib_copy = remote(own_q.at[core], own_q.at[core], sib_sem.at[0], sib_sem.at[1], sibling)
     sib_copy.start()
     w_copy = remote(my_cols, my_cols, w_sem.at[0], w_sem.at[1], sibling)
     w_copy.start()
-    other_rows = pl.ds(pl.multiple_of(8 - core * 8, 8), 8)
-    remote(own_q.at[:, other_rows, :], own_q.at[:, other_rows, :], sib_sem.at[0], sib_sem.at[1], sibling).wait_recv()
-    queries[0, chip] = own_q[...].reshape(BLOCK, HD).astype(BF16)
-    zq_copy = remote(queries.at[0, chip], queries.at[1, chip], zq_sem.at[0], zq_sem.at[1], zh_peer)
-    zq_copy.start()
+
+    def assemble(rel, pair):
+        for j in range(GROUP):
+            at = (slice(j // 3 * 8, j // 3 * 8 + 8), slice(j % 3 * HD, j % 3 * HD + HD))
+            rows = jnp.concatenate([pair[k][at].astype(F32) for k in range(2)], axis=0)
+            queries[rel, chip, j * 16 : (j + 1) * 16, :] = rows.astype(BF16)
+
+    remote(own_q.at[1 - core], own_q.at[1 - core], sib_sem.at[0], sib_sem.at[1], sibling).wait_recv()
+    assemble(0, [own_q[0], own_q[1]])
 
     def send_queries(rel):
         for i in range(1, 16):
@@ -156,7 +167,7 @@
     start = (seq * shard_len).astype(F32)
 
     def chunk(g, _):
-        rel, t = g // 4, (g + g // 4) % 4
+        rel, t = g // 4, g % 4
         row_y = (y + t + t // 2 - 2 * (t // 3)) % 4
         zh_of = (zh + rel) % 2
 
@@ -212,10 +223,11 @@
         lax.fori_loop(0, 4, depart, 0)
         return 0
 
-    lax.fori_loop(0, 3, chunk, 0)
-    zq_copy.wait()
+    for side in range(2):
+        remote(far_q.at[side], far_q.at[side], zq_send.at[side], zq_recv.at[side], sibling).wait_recv()
+    assemble(1, [far_q[0], far_q[1]])
     send_queries(1)
-    lax.fori_loop(3, 8, chunk, 0)
+    lax.fori_loop(0, 8, chunk, 0)
 
     all_parts = remote(partial.at[pl.ds(0, 31)], landed.at[pl.ds(0, 31)], part_sem.at[0], part_sem.at[1], sibling)
     all_parts.wait_recv()
@@ -309,6 +321,8 @@
     out_ref[...] = result[:, :cols].astype(BF16)
 
     sib_copy.wait_send()
+    for copy in zh_copies:
+        copy.wait_send()
     for rel in range(2):
         some = queries.at[rel, pl.ds(0, 15)]
         remote(some, some, q_send.at[rel], q_recv.at[rel, 0], sibling).wait_send()
@@ -332,7 +346,8 @@
         scratch_shapes=[
             pltpu.VMEM((shard_len, HD), BF16),
             pltpu.VMEM((shard_len, HD), BF16),
-            pltpu.VMEM((GROUP, 16, HD), F32),
+            pltpu.VMEM((2, 16, 3 * HD), BF16),
+            pltpu.VMEM((2, 16, 3 * HD), BF16),
             pltpu.VMEM((2, 16, BLOCK, HD), BF16),
             pltpu.VMEM((2 * HD, shard_len), BF16),
             pltpu.VMEM((shard_len, 2 * HD), BF16),
@@ -356,6 +371,7 @@
             dma((2,)),
             dma((2,)),
             dma((2,)),
+            dma((2,)),
             dma((2, 4)),
             dma((2,)),
             dma((2,)),

time: 68.7 us -> 64.8 us (0.943)
  Pallas kernels: 67.1 us -> 63.2 us
    pallas_call x1, Pallas kernels: 67.1 us -> 63.2 us  [shards(): pl.pallas_call(kernel, out_shape=jax.ShapeDtypeStruct((64, cols), BF16),...]
where the time goes in v3:
time: 64.8 us; the launch traced here: 64.5 us
  Pallas kernels  63.2 us (98%)
  local copies, waits for them, and re-layouts  1.32 us (2%)
    pallas_call x1, Pallas kernels, shards(): pl.pallas_call(kernel, out_shape=jax.ShapeDtypeStruct((64, cols), BF16),...  63.2 us
    unnamed x1, local copies, waits for them, and re-layouts  1.32 us

profile of v3, /device:TPU:9, one launch (start us, length us, event | category | flops | bytes accessed | tf_op | source)
XLA Modules:
  0.0 64.5 jit_solution(7092776230819944322)
XLA Ops:
  0.0 63.2 %tracing.1 = bf16[64,80]{1,0:T(8,128)(2,1)} custom-call(bf16[8,640]{1,0:T(8,128)(2,1)} %cq_ref.1, bf16[8,640]{1,0:T(8,128)(2,1)} %nz_ref.1, bf16[2048,128]{1,0:T(8,128)(2,1)} %k_hbm.1, bf16[2048,128]{1,0:T(8,128)(2,1)} %v_hbm.1, bf16[80,640]{1,0:T(8,128)(2,1)} %bitcast.3, s32[4,128]{1,0:T(4,128)} %bitcast.4, s32[4,128]{1,0:T(4,128)} %bitcast.5, s32[16]{0:T(128)} %restored_ref.1), custom_call_target="tpu_custom_call" | custom-call | tf_op jit(solution)/shard_map/tracing/pallas_call | solution.py:341
  63.2 1.3 %copy.10 = bf16[64,80]{1,0:T(8,128)(2,1)} copy(bf16[64,80]{1,0:T(8,128)(2,1)} %tracing.1) | data formatting | bytes 20480

commit v4 on v3

--- a/solution.py
+++ b/solution.py
@@ -267,7 +267,7 @@
         ].astype(F32)
         attended[chip, j * 16 : (j + 1) * 16, :] = mixed.astype(BF16)
 
-    for i in range(1, 16):
+    for i in range(15, 0, -1):
         remote(
             attended.at[chip], attended.at[chip], att_send.at[0], att_recv.at[y],
             device(zh, plane_chip(i), core, head),

time: 64.8 us -> 66.1 us (1.020)
  the two profiles are of different devices: /device:TPU:9 before, /device:TPU:1 now
where the time goes in v4:
time: 66.1 us; the launch traced here: 65.9 us
  Pallas kernels  64.5 us (98%)
  local copies, waits for them, and re-layouts  1.32 us (2%)
    pallas_call x1, Pallas kernels, shards(): pl.pallas_call(kernel, out_shape=jax.ShapeDtypeStruct((64, cols), BF16),...  64.5 us
    unnamed x1, local copies, waits for them, and re-layouts  1.32 us

profile of v4, /device:TPU:1, one launch (start us, length us, event | category | flops | bytes accessed | tf_op | source)
XLA Modules:
  0.0 65.9 jit_solution(16820411362277812871)
XLA Ops:
  0.0 64.5 %tracing.1 = bf16[64,80]{1,0:T(8,128)(2,1)} custom-call(bf16[8,640]{1,0:T(8,128)(2,1)} %cq_ref.1, bf16[8,640]{1,0:T(8,128)(2,1)} %nz_ref.1, bf16[2048,128]{1,0:T(8,128)(2,1)} %k_hbm.1, bf16[2048,128]{1,0:T(8,128)(2,1)} %v_hbm.1, bf16[80,640]{1,0:T(8,128)(2,1)} %bitcast.3, s32[4,128]{1,0:T(4,128)} %bitcast.4, s32[4,128]{1,0:T(4,128)} %bitcast.5, s32[16]{0:T(128)} %restored_ref.1), custom_call_target="tpu_custom_call" | custom-call | tf_op jit(solution)/shard_map/tracing/pallas_call | solution.py:341
  64.5 1.3 %copy.10 = bf16[64,80]{1,0:T(8,128)(2,1)} copy(bf16[64,80]{1,0:T(8,128)(2,1)} %tracing.1) | data formatting | bytes 20480

commit v5 on v3

--- a/solution.py
+++ b/solution.py
@@ -204,7 +204,7 @@
                     )
 
         def depart(i, _):
-            owner = row_y * 4 + i
+            owner = row_y * 4 + lax.rem(x + 2 + i, 4)
             mine = (owner == chip) & (zh_of == core)
 
             @pl.when(mine)

time: 64.8 us -> 64.8 us (level)
  no operation moved by 1% of the time
where the time goes in v5:
time: 64.8 us; the launch traced here: 64.5 us
  Pallas kernels  63.2 us (98%)
  local copies, waits for them, and re-layouts  1.32 us (2%)
    pallas_call x1, Pallas kernels, shards(): pl.pallas_call(kernel, out_shape=jax.ShapeDtypeStruct((64, cols), BF16),...  63.2 us
    unnamed x1, local copies, waits for them, and re-layouts  1.32 us

profile of v5, /device:TPU:9, one launch (start us, length us, event | category | flops | bytes accessed | tf_op | source)
XLA Modules:
  0.0 64.5 jit_solution(18214599992531339302)
XLA Ops:
  0.0 63.2 %tracing.1 = bf16[64,80]{1,0:T(8,128)(2,1)} custom-call(bf16[8,640]{1,0:T(8,128)(2,1)} %cq_ref.1, bf16[8,640]{1,0:T(8,128)(2,1)} %nz_ref.1, bf16[2048,128]{1,0:T(8,128)(2,1)} %k_hbm.1, bf16[2048,128]{1,0:T(8,128)(2,1)} %v_hbm.1, bf16[80,640]{1,0:T(8,128)(2,1)} %bitcast.3, s32[4,128]{1,0:T(4,128)} %bitcast.4, s32[4,128]{1,0:T(4,128)} %bitcast.5, s32[16]{0:T(128)} %restored_ref.1), custom_call_target="tpu_custom_call" | custom-call | tf_op jit(solution)/shard_map/tracing/pallas_call | solution.py:341
  63.2 1.3 %copy.10 = bf16[64,80]{1,0:T(8,128)(2,1)} copy(bf16[64,80]{1,0:T(8,128)(2,1)} %tracing.1) | data formatting | bytes 20480
